TPU v7x, 512 devices: a whole 4x8x8 slice. The times are simulated.
512 devices in a mesh: dp: 8 (over z), seq: 64 (over y, x, core).
Axes of the slice: x: 4, y: 8, z: 8, core: 2. Of those that a mesh axis runs over, the one named last changes fastest.
Arguments:
- tokens: bfloat16 [8, 8192, 1280], P('dp', 'seq'), may hold values from -6 to 6
- place: int32 [64, 128], P('seq'), may hold values from 0 to 127, each once within a row
- kernel: float32 [27, 1280], replicated, may hold values from -1.25 to 1.25
- proj_weight: bfloat16 [1280, 3840], P('seq'), may hold values from -0.15625 to 0.15625
- d_projected: bfloat16 [8, 8192, 3840], P('dp', 'seq'), may hold values from -6 to 6
Outputs:
- projected: bfloat16 [8, 8192, 3840], P('dp', 'seq')
- d_tokens: bfloat16 [8, 8192, 1280], P('dp', 'seq')
- d_kernel: float32 [27, 1280], replicated
Inputs may be any that keep to these rules, and one draw needn't show every extreme that they name: Each row of place holds every number 0 to 127 once.
All inputs are finite; a program needn't handle non-finite values.
Results may differ from a plain program's by a relative error of at most 0.005.
Values may be sent and summed in bfloat16 or wider, within the bound.
No kernel may reach another device: no remote copies, remote signals or barrier semaphores. Data moves between devices by JAX's collectives and lax.ppermute only.
A program may use at most 128 MiB of HBM per device.

v0:
```python
import jax
import jax.numpy as jnp
from jax import lax
from jax.sharding import PartitionSpec as P

INLINE = 8
CROSS = 8


def with_halo(value, sides, width):
    for axis, dim in sides:
        size, length = (lax.axis_size(axis), value.shape[dim])
        up = [(i, (i + 1) % size) for i in range(size - 1)]
        down = [(j, i) for i, j in up]
        last = lax.slice_in_dim(value, length - width, length, axis=dim)
        first = lax.slice_in_dim(value, 0, width, axis=dim)
        before = lax.ppermute(last, axis, up)
        after = lax.ppermute(first, axis, down)
        value = jnp.concatenate([before, value, after], axis=dim)
    return value


def brick_cells(landed, inverse):
    tokens_dev = inverse.shape[0]
    width = landed.shape[-1]
    slots = landed.reshape(tokens_dev, width)
    cells = jnp.take(slots, inverse, axis=0)
    return cells.reshape(tokens_dev // (INLINE * CROSS), INLINE, CROSS, width)


def scan_pieces(cells, order, count):
    width = cells.shape[-1]
    tokens_dev = order.shape[0]
    slots = jnp.take(cells.reshape(tokens_dev, width), order, axis=0)
    return slots.reshape(count, tokens_dev // count, width)


def to_bricks(rows, inverse, count):
    tokens_dev, width = rows.shape
    landed = lax.all_to_all(
        rows.reshape(count, tokens_dev // count, width),
        "seq",
        split_axis=0,
        concat_axis=0,
        tiled=True,
    )
    return brick_cells(landed, inverse)


def to_scan(cells, order, count):
    landed = lax.all_to_all(
        scan_pieces(cells, order, count), "seq", split_axis=0, concat_axis=0, tiled=True
    )
    return landed.reshape(order.shape[0], cells.shape[-1])


def with_faces(block):
    deeper = with_halo(block, (("seq", 0),), 1)
    return jnp.pad(deeper, ((0, 0), (1, 1), (1, 1), (0, 0)))


def window(field, depth_dev, start_z, start_i, start_c):
    return field[
        start_z : start_z + depth_dev, start_i : start_i + INLINE, start_c : start_c + CROSS
    ].astype(jnp.float32)


def forward_conv(grid_x, pad_x, kernel, depth_dev):
    conv = jnp.zeros(grid_x.shape, jnp.float32)
    for offset in range(27):
        conv = conv + kernel[offset] * window(
            pad_x, depth_dev, offset // 9, offset // 3 % 3, offset % 3
        )
    return (grid_x.astype(jnp.float32) + conv).astype(jnp.bfloat16)


def backward_conv(grid_d, pad_d, pad_x, kernel, depth_dev):
    grid_float = grid_d.astype(jnp.float32)
    back = grid_float
    partial_value = []
    for offset in range(27):
        dz, di, dc = (offset // 9, offset // 3 % 3, offset % 3)
        back = back + kernel[offset] * window(pad_d, depth_dev, 2 - dz, 2 - di, 2 - dc)
        partial_value.append(
            jnp.sum(grid_float * window(pad_x, depth_dev, dz, di, dc), axis=(0, 1, 2))
        )
    return (back.astype(jnp.bfloat16), jnp.stack(partial_value))


def shards(tokens, place, kernel, proj_weight, d_projected):
    count = lax.axis_size("seq")
    order = place[0]
    inverse = jnp.argsort(order)
    rows_x = tokens[0]
    d_rows = d_projected[0]
    depth_dev = rows_x.shape[0] // (INLINE * CROSS)
    d_y = lax.dot_general(
        d_rows,
        lax.all_gather(proj_weight, "seq", axis=0, tiled=True),
        (((1,), (1,)), ((), ())),
        preferred_element_type=jnp.float32,
    )
    d_y = d_y.astype(jnp.bfloat16)
    grid_x = to_bricks(rows_x, inverse, count)
    pad_x = with_faces(grid_x)
    grid_y = forward_conv(grid_x, pad_x, kernel, depth_dev)
    rows_y = to_scan(grid_y, order, count)
    grid_d = to_bricks(d_y, inverse, count)
    pad_d = with_faces(grid_d)
    back, partial_value = backward_conv(grid_d, pad_d, pad_x, kernel, depth_dev)
    d_tokens = to_scan(back, order, count)
    projected = jnp.dot(
        rows_y,
        lax.all_gather(proj_weight, "seq", axis=0, tiled=True),
        preferred_element_type=jnp.float32,
    )
    projected = projected.astype(jnp.bfloat16)
    d_kernel = lax.psum(partial_value, ("dp", "seq"))
    return (projected[None], d_tokens[None], d_kernel)


def solution(mesh):
    placed = (P("dp", "seq", None), P("seq", None), P(), P("seq", None), P("dp", "seq", None))
    return jax.shard_map(
        shards,
        mesh=mesh,
        in_specs=placed,
        out_specs=(P("dp", "seq", None), P("dp", "seq", None), P()),
        check_vma=False,
    )
```

profile of v0, /device:TPU:1, one launch (start us, length us, event | category | flops | bytes accessed | tf_op | source)
XLA Modules:
  0.0 491.7 jit_solution(6049392206160936502)
XLA Ops:
  7.9 1.8 reshape_squeeze.3
  9.7 11.6 %all-to-all-start = ((bf16[64,2,1280]{2,1,0:T(2,128)(2,1)}), bf16[64,2,1280]{2,1,0:T(2,128)(2,1)S(1)}, u32[]{:S(2)}, u32[]{:S(2)}) async-start(bf16[64,2,1280]{2,1,0:T(2,128)(2,1)} %reshape_squeeze.3), calls=%async_computation | async-start | bytes 655360 | tf_op jit(solution)/shard_map/all_to_all | solution.py:40
  21.4 3.2 sort.17
  24.6 1.9 slice_reduce_fusion.25
  27.1 83.8 %all-gather.3.cloned.1.call-done = bf16[64,20,3840]{2,1,0:T(8,128)(2,1)} async-done(((bf16[1,20,3840]{2,1,0:T(8,128)(2,1)}), bf16[64,20,3840]{2,1,0:T(8,128)(2,1)}) %all-gather.3.cloned.1.call-update) | async-done | bytes 9830416 | tf_op jit(solution)/shard_map/all_gather | solution.py:114
  110.9 13.7 %reshape.119 = bf16[1280,3840]{1,0:T(8,128)(2,1)} reshape(bf16[64,20,3840]{2,1,0:T(8,128)(2,1)} %all-gather.3.cloned.1.call-done) | data formatting | bytes 19660800
  124.6 7.1 %convolution_convert_fusion.1 = bf16[128,1280]{1,0:T(8,128)(2,1)S(1)} fusion(bf16[1280,3840]{1,0:T(8,128)(2,1)} %reshape.119, bf16[1,128,3840]{2,1,0:T(8,128)(2,1)S(1)} %copy-done), kind=kOutput, calls=%fused_computation.41 | convolution fusion | flops 1258455040 | bytes 11141120 | tf_op jit(solution)/shard_map/dot_general | solution.py:97
  132.6 5.7 %all-to-all-start.2 = ((bf16[64,2,1280]{2,1,0:T(2,128)(2,1)}), bf16[64,2,1280]{2,1,0:T(2,128)(2,1)S(1)}, u32[]{:S(2)}, u32[]{:S(2)}) async-start(bf16[64,2,1280]{2,1,0:T(2,128)(2,1)} %reshape.77), calls=%async_computation.2 | async-start | bytes 655360 | tf_op jit(solution)/shard_map/all_to_all | solution.py:40
  141.2 11.2 %all-to-all-done.2 = bf16[64,2,1280]{2,1,0:T(2,128)(2,1)S(1)} async-done(((bf16[64,2,1280]{2,1,0:T(2,128)(2,1)}), bf16[64,2,1280]{2,1,0:T(2,128)(2,1)S(1)}, u32[]{:S(2)}, u32[]{:S(2)}) %all-to-all-start.2) | async-done | bytes 327712 | tf_op jit(solution)/shard_map/all_to_all | solution.py:40
  152.6 0.9 gather_fusion.2
  154.4 2.1 collective-permute-start.1
  156.5 3.5 collective-permute-start
  160.7 1.9 collective-permute-start.2
  162.7 3.1 collective-permute-start.3
  166.5 2.5 fusion.83
  169.0 1.7 gather_fusion.1
  170.7 1.5 select_maximum_fusion
  172.2 3.4 add_convert_fusion
  175.7 1.9 gather_fusion.3
  177.5 1.9 broadcast_select_fusion
  179.5 1.8 reshape.75
  181.3 9.7 %all-to-all-start.1 = ((bf16[64,2,1280]{2,1,0:T(2,128)(2,1)}), bf16[64,2,1280]{2,1,0:T(2,128)(2,1)}, u32[]{:S(2)}, u32[]{:S(2)}) async-start(bf16[64,2,1280]{2,1,0:T(2,128)(2,1)} %reshape.75), calls=%async_computation.1 | async-start | bytes 655360 | tf_op jit(solution)/shard_map/all_to_all | solution.py:51
  192.4 2.4 fusion.82
  194.8 10.2 %all-to-all-done.1 = bf16[64,2,1280]{2,1,0:T(2,128)(2,1)} async-done(((bf16[64,2,1280]{2,1,0:T(2,128)(2,1)}), bf16[64,2,1280]{2,1,0:T(2,128)(2,1)}, u32[]{:S(2)}, u32[]{:S(2)}) %all-to-all-start.1) | async-done | bytes 327712 | tf_op jit(solution)/shard_map/all_to_all | solution.py:51
  205.0 5.2 %all-to-all-start.3 = ((bf16[64,2,1280]{2,1,0:T(2,128)(2,1)}), bf16[64,2,1280]{2,1,0:T(2,128)(2,1)}, u32[]{:S(2)}, u32[]{:S(2)}) async-start(bf16[64,2,1280]{2,1,0:T(2,128)(2,1)} %reshape.81), calls=%async_computation.3 | async-start | bytes 655360 | tf_op jit(solution)/shard_map/all_to_all | solution.py:51
  210.3 1.5 fusion.78
  215.0 3.4 stack.111
  218.4 1.1 reshape.76
  219.5 6.2 %fusion = bf16[1,128,3840]{2,1,0:T(8,128)(2,1)} fusion(bf16[128,1280]{1,0:T(8,128)(2,1)S(1)} %reshape.76, bf16[1280,3840]{1,0:T(8,128)(2,1)} %reshape.119), kind=kOutput, calls=%fused_computation.37 | convolution fusion | flops 1258782720 | bytes 11141120 | tf_op jit(solution)/shard_map/dot_general | solution.py:112
  225.7 1.8 broadcast_in_dim_reshape.3
  227.5 255.8 %all-reduce.4.cloned.1.call-done = f32[27,1280]{1,0:T(8,128)} async-done(((f32[27,1280]{1,0:T(8,128)}), f32[27,1280]{1,0:T(8,128)}) %all-reduce.4.cloned.1.call-update) | async-done | bytes 138256 | tf_op jit(solution)/shard_map/psum | solution.py:118
  483.3 1.6 copy.9
  (94 shorter events, 12.0 us)
Async XLA Ops:
  7.2 117.5 %copy-start = (bf16[1,128,3840]{2,1,0:T(8,128)(2,1)S(1)}, bf16[1,128,3840]{2,1,0:T(8,128)(2,1)}, u32[]{:S(2)}) copy-start(bf16[1,128,3840]{2,1,0:T(8,128)(2,1)} %param.11) | copy-start | bytes 2949124
  7.2 103.8 %all-gather.3.cloned.1.call-start = ((), (), s32[]{:S(2)}) async-start(), calls=%async_computation.5 | async-start | bytes 11980800 | tf_op jit(solution)/shard_map/all_gather | solution.py:114
  9.7 122.8 %all-to-all-start = ((bf16[64,2,1280]{2,1,0:T(2,128)(2,1)}), bf16[64,2,1280]{2,1,0:T(2,128)(2,1)S(1)}, u32[]{:S(2)}, u32[]{:S(2)}) async-start(bf16[64,2,1280]{2,1,0:T(2,128)(2,1)} %reshape_squeeze.3), calls=%async_computation | async-start | bytes 655360 | tf_op jit(solution)/shard_map/all_to_all | solution.py:40
  124.6 14.2 %copy-start.4 = (f32[27,1280]{1,0:T(8,128)S(1)}, f32[27,1280]{1,0:T(8,128)}, u32[]{:S(2)}) copy-start(f32[27,1280]{1,0:T(8,128)} %param.9) | copy-start | bytes 414724
  124.6 15.1 %copy-start.19 = (s32[1,128]{1,0:T(1,128)S(1)}, s32[1,128]{1,0:T(1,128)}, u32[]{:S(2)}) copy-start(s32[1,128]{1,0:T(1,128)} %param.8) | copy-start | bytes 1540
  132.6 19.9 %all-to-all-start.2 = ((bf16[64,2,1280]{2,1,0:T(2,128)(2,1)}), bf16[64,2,1280]{2,1,0:T(2,128)(2,1)S(1)}, u32[]{:S(2)}, u32[]{:S(2)}) async-start(bf16[64,2,1280]{2,1,0:T(2,128)(2,1)} %reshape.77), calls=%async_computation.2 | async-start | bytes 655360 | tf_op jit(solution)/shard_map/all_to_all | solution.py:40
  153.5 12.9 %copy-start.5 = (f32[1280]{0:T(1024)S(1)}, f32[1280]{0:T(1024)}, u32[]{:S(2)}) copy-start(f32[1280]{0:T(1024)} %get-tuple-element.52) | copy-start | bytes 15364
  153.5 12.9 %copy-start.6 = (f32[1280]{0:T(1024)S(1)}, f32[1280]{0:T(1024)}, u32[]{:S(2)}) copy-start(f32[1280]{0:T(1024)} %get-tuple-element.53) | copy-start | bytes 15364
  153.5 12.9 %copy-start.7 = (f32[1280]{0:T(1024)S(1)}, f32[1280]{0:T(1024)}, u32[]{:S(2)}) copy-start(f32[1280]{0:T(1024)} %get-tuple-element.54) | copy-start | bytes 15364
  153.5 12.9 %copy-start.8 = (f32[1280]{0:T(1024)S(1)}, f32[1280]{0:T(1024)}, u32[]{:S(2)}) copy-start(f32[1280]{0:T(1024)} %get-tuple-element.55) | copy-start | bytes 15364
  153.5 12.9 %copy-start.9 = (f32[1280]{0:T(1024)S(1)}, f32[1280]{0:T(1024)}, u32[]{:S(2)}) copy-start(f32[1280]{0:T(1024)} %get-tuple-element.56) | copy-start | bytes 15364
  153.5 12.9 %copy-start.10 = (f32[1280]{0:T(1024)S(1)}, f32[1280]{0:T(1024)}, u32[]{:S(2)}) copy-start(f32[1280]{0:T(1024)} %get-tuple-element.57) | copy-start | bytes 15364
  153.5 12.9 %copy-start.11 = (f32[1280]{0:T(1024)S(1)}, f32[1280]{0:T(1024)}, u32[]{:S(2)}) copy-start(f32[1280]{0:T(1024)} %get-tuple-element.58) | copy-start | bytes 15364
  153.5 12.9 %copy-start.12 = (f32[1280]{0:T(1024)S(1)}, f32[1280]{0:T(1024)}, u32[]{:S(2)}) copy-start(f32[1280]{0:T(1024)} %get-tuple-element.59) | copy-start | bytes 15364
  153.5 12.9 %copy-start.13 = (f32[1280]{0:T(1024)S(1)}, f32[1280]{0:T(1024)}, u32[]{:S(2)}) copy-start(f32[1280]{0:T(1024)} %get-tuple-element.60) | copy-start | bytes 15364
  153.6 12.9 %copy-start.14 = (f32[1280]{0:T(1024)S(1)}, f32[1280]{0:T(1024)}, u32[]{:S(2)}) copy-start(f32[1280]{0:T(1024)} %get-tuple-element.61) | copy-start | bytes 15364
  153.6 12.9 %copy-start.15 = (f32[1280]{0:T(1024)S(1)}, f32[1280]{0:T(1024)}, u32[]{:S(2)}) copy-start(f32[1280]{0:T(1024)} %get-tuple-element.62) | copy-start | bytes 15364
  153.6 12.9 %copy-start.16 = (f32[1280]{0:T(1024)S(1)}, f32[1280]{0:T(1024)}, u32[]{:S(2)}) copy-start(f32[1280]{0:T(1024)} %get-tuple-element.63) | copy-start | bytes 15364
  153.6 12.9 %copy-start.17 = (f32[1280]{0:T(1024)S(1)}, f32[1280]{0:T(1024)}, u32[]{:S(2)}) copy-start(f32[1280]{0:T(1024)} %get-tuple-element.64) | copy-start | bytes 15364
  154.4 14.5 %copy-start.1 = (bf16[128,1280]{1,0:T(8,128)(2,1)}, bf16[128,1280]{1,0:T(8,128)(2,1)S(1)}, u32[]{:S(2)}) copy-start(bf16[128,1280]{1,0:T(8,128)(2,1)S(1)} %get-tuple-element.67) | copy-start | bytes 983044
  154.4 11.3 %collective-permute-start.1 = (bf16[1,8,8,1280]{3,2,1,0:T(8,128)(2,1)S(1)}, bf16[1,8,8,1280]{3,2,1,0:T(8,128)(2,1)S(1)}, u32[]{:S(2)}, u32[]{:S(2)}) collective-permute-start(bf16[1,8,8,1280]{3,2,1,0:T(8,128)(2,1)S(1)} %get-tuple-element.70), channel_id=1, source_target_pairs={{1,0},{2,1},{3,2},{4,3},{5,4},{6,5},{7,6},{8,7},{9,8},{10,9},{11,1... | collective-permute-start | bytes 491528 | tf_op jit(solution)/shard_map/ppermute | solution.py:18
  156.5 9.2 %collective-permute-start = (bf16[1,8,8,1280]{3,2,1,0:T(8,128)(2,1)S(1)}, bf16[1,8,8,1280]{3,2,1,0:T(8,128)(2,1)S(1)}, u32[]{:S(2)}, u32[]{:S(2)}) collective-permute-start(bf16[1,8,8,1280]{3,2,1,0:T(8,128)(2,1)S(1)} %get-tuple-element.71), channel_id=1, source_target_pairs={{0,1},{1,2},{2,3},{3,4},{4,5},{5,6},{6,7},{7,8},{8,9},{9,10},{10,1... | collective-permute-start | bytes 491528 | tf_op jit(solution)/shard_map/ppermute | solution.py:17
  160.7 10.0 %collective-permute-start.2 = (bf16[1,8,8,1280]{3,2,1,0:T(8,128)(2,1)}, bf16[1,8,8,1280]{3,2,1,0:T(8,128)(2,1)}, u32[]{:S(2)}, u32[]{:S(2)}) collective-permute-start(bf16[1,8,8,1280]{3,2,1,0:T(8,128)(2,1)} %get-tuple-element.68), channel_id=1, source_target_pairs={{0,1},{1,2},{2,3},{3,4},{4,5},{5,6},{6,7},{7,8},{8,9},{9,10},{10,1... | collective-permute-start | bytes 491528 | tf_op jit(solution)/shard_map/ppermute | solution.py:17
  162.7 8.0 %collective-permute-start.3 = (bf16[1,8,8,1280]{3,2,1,0:T(8,128)(2,1)}, bf16[1,8,8,1280]{3,2,1,0:T(8,128)(2,1)}, u32[]{:S(2)}, u32[]{:S(2)}) collective-permute-start(bf16[1,8,8,1280]{3,2,1,0:T(8,128)(2,1)} %get-tuple-element.69), channel_id=1, source_target_pairs={{1,0},{2,1},{3,2},{4,3},{5,4},{6,5},{7,6},{8,7},{9,8},{10,9},{11,1... | collective-permute-start | bytes 491528 | tf_op jit(solution)/shard_map/ppermute | solution.py:18
  165.7 3.2 copy-start.3
  175.6 15.3 %copy-start.18 = (f32[1280]{0:T(1024)S(1)}, f32[1280]{0:T(1024)}, u32[]{:S(2)}) copy-start(f32[1280]{0:T(1024)} %get-tuple-element.65) | copy-start | bytes 15364
  181.3 23.8 %all-to-all-start.1 = ((bf16[64,2,1280]{2,1,0:T(2,128)(2,1)}), bf16[64,2,1280]{2,1,0:T(2,128)(2,1)}, u32[]{:S(2)}, u32[]{:S(2)}) async-start(bf16[64,2,1280]{2,1,0:T(2,128)(2,1)} %reshape.75), calls=%async_computation.1 | async-start | bytes 655360 | tf_op jit(solution)/shard_map/all_to_all | solution.py:51
  192.4 18.0 %copy-start.2 = (bf16[128,1280]{1,0:T(8,128)(2,1)S(1)}, bf16[128,1280]{1,0:T(8,128)(2,1)}, u32[]{:S(2)}) copy-start(bf16[128,1280]{1,0:T(8,128)(2,1)} %copy-done.1) | copy-start | bytes 983044
  205.0 20.6 %all-to-all-start.3 = ((bf16[64,2,1280]{2,1,0:T(2,128)(2,1)}), bf16[64,2,1280]{2,1,0:T(2,128)(2,1)}, u32[]{:S(2)}, u32[]{:S(2)}) async-start(bf16[64,2,1280]{2,1,0:T(2,128)(2,1)} %reshape.81), calls=%async_computation.3 | async-start | bytes 655360 | tf_op jit(solution)/shard_map/all_to_all | solution.py:51
  210.3 273.0 %all-reduce.4.cloned.1.call-start = ((), (), s32[]{:S(2)}) async-start(), calls=%async_computation.4 | async-start | bytes 327680 | tf_op jit(solution)/shard_map/psum | solution.py:118
Sparse Core Ops, SparseCore 0:
  11.3 99.6 all-gather.2
  218.5 264.7 all-reduce.3
where the time goes:
time: 493 us; the launch traced here: 492 us
  waiting for transfers between devices  362 us (73%)
  starting transfers between devices  42.8 us (9%)
  local copies, waits for them, and re-layouts  39.6 us (8%)
  other arithmetic  19.6 us (4%)
  between operations  14.6 us (3%)
  matrix products  13.3 us (3%)
    psum x1, waiting for transfers between devices, shards(): d_kernel = lax.psum(partial_value, ('dp', 'seq'))  256 us
    all_gather x1, waiting for transfers between devices, shards(): lax.all_gather(proj_weight, 'seq', axis=0, tiled=True)  83.8 us
    all_to_all x2, starting transfers between devices, to_bricks(): lax.all_to_all(rows.reshape(count, tokens_dev // count, width), 'seq', sp...  17.3 us
    unnamed x42, local copies, waits for them, and re-layouts  15.4 us
    all_to_all x2, starting transfers between devices, to_scan(): lax.all_to_all(scan_pieces(cells, order, count), 'seq', split_axis=0, con...  14.9 us
    all_to_all x2, waiting for transfers between devices, to_bricks(): lax.all_to_all(rows.reshape(count, tokens_dev // count, width), 'seq', sp...  11.2 us
    all_to_all x2, waiting for transfers between devices, to_scan(): lax.all_to_all(scan_pieces(cells, order, count), 'seq', split_axis=0, con...  10.3 us
  transfers between devices with their start and end apart: 10, of which 4 were waited for; matrix products, arithmetic and copies ran while one was open for 12% of the time, Pallas kernels for 0%

commit v1 on v0

--- a/solution.py
+++ b/solution.py
@@ -115,7 +115,7 @@
         preferred_element_type=jnp.float32,
     )
     projected = projected.astype(jnp.bfloat16)
-    d_kernel = lax.psum(partial_value, ("dp", "seq"))
+    d_kernel = jnp.sum(lax.all_gather(partial_value, ("dp", "seq")), axis=0)
     return (projected[None], d_tokens[None], d_kernel)
 
 

time: 493 us -> 457 us (0.927)
  waiting for transfers between devices: 362 us -> 311 us
  other arithmetic: 19.6 us -> 41.1 us
  local copies, waits for them, and re-layouts: 39.6 us -> 27 us
  starting transfers between devices: 42.8 us -> 49.2 us
    psum x1 -> x0, waiting for transfers between devices: 256 us -> none  [shards(): d_kernel = lax.psum(partial_value, ('dp', 'seq'))]
    all_gather x0 -> x1, waiting for transfers between devices: none -> 174 us  [shards(): d_kernel = jnp.sum(lax.all_gather(partial_value, ('dp', 'seq')), axis=0)]
    reduce_sum x0 -> x1, other arithmetic: none -> 26.7 us  [shards(): d_kernel = jnp.sum(lax.all_gather(partial_value, ('dp', 'seq')), axis=0)]
    all_to_all x2, waiting for transfers between devices: 10.3 us -> 29.9 us  [to_scan(): lax.all_to_all(scan_pieces(cells, order, count), 'seq', split_axis=0, con...]
    all_to_all x2, starting transfers between devices: 14.9 us -> 21.3 us  [to_scan(): lax.all_to_all(scan_pieces(cells, order, count), 'seq', split_axis=0, con...]
    all_gather x1, waiting for transfers between devices: 83.8 us -> 89.6 us  [shards(): lax.all_gather(proj_weight, 'seq', axis=0, tiled=True)]
    unnamed x42 -> x39, local copies, waits for them, and re-layouts: 15.4 us -> 13.7 us
  transfers between devices with their start and end apart: 10 -> 10, of which waited for: 4 -> 8; matrix products, arithmetic and copies ran while one was open for 12% -> 10% of each run, Pallas kernels for 0% -> 0%
where the time goes in v1:
time: 457 us; the launch traced here: 456 us
  waiting for transfers between devices  311 us (68%)
  starting transfers between devices  49.2 us (11%)
  other arithmetic  41.1 us (9%)
  local copies, waits for them, and re-layouts  27 us (6%)
  between operations  14.7 us (3%)
  matrix products  13.4 us (3%)
    all_gather x1, waiting for transfers between devices, shards(): d_kernel = jnp.sum(lax.all_gather(partial_value, ('dp', 'seq')), axis=0)  174 us
    all_gather x1, waiting for transfers between devices, shards(): lax.all_gather(proj_weight, 'seq', axis=0, tiled=True)  89.6 us
    all_to_all x2, waiting for transfers between devices, to_scan(): lax.all_to_all(scan_pieces(cells, order, count), 'seq', split_axis=0, con...  29.9 us
    reduce_sum x1, other arithmetic, shards(): d_kernel = jnp.sum(lax.all_gather(partial_value, ('dp', 'seq')), axis=0)  26.7 us
    all_to_all x2, starting transfers between devices, to_scan(): lax.all_to_all(scan_pieces(cells, order, count), 'seq', split_axis=0, con...  21.3 us
    all_to_all x2, starting transfers between devices, to_bricks(): lax.all_to_all(rows.reshape(count, tokens_dev // count, width), 'seq', sp...  17.3 us
    unnamed x39, local copies, waits for them, and re-layouts  13.7 us
    all_to_all x2, waiting for transfers between devices, to_bricks(): lax.all_to_all(rows.reshape(count, tokens_dev // count, width), 'seq', sp...  10.5 us
  transfers between devices with their start and end apart: 10, of which 8 were waited for; matrix products, arithmetic and copies ran while one was open for 10% of the time, Pallas kernels for 0%

profile of v1, /device:TPU:1, one launch (start us, length us, event | category | flops | bytes accessed | tf_op | source)
XLA Modules:
  0.0 455.9 jit_solution(2375060246221415462)
XLA Ops:
  7.9 1.8 reshape_squeeze.3
  9.7 11.6 %all-to-all-start = ((bf16[64,2,1280]{2,1,0:T(2,128)(2,1)}), bf16[64,2,1280]{2,1,0:T(2,128)(2,1)S(1)}, u32[]{:S(2)}, u32[]{:S(2)}) async-start(bf16[64,2,1280]{2,1,0:T(2,128)(2,1)} %reshape_squeeze.3), calls=%async_computation | async-start | bytes 655360 | tf_op jit(solution)/shard_map/all_to_all | solution.py:40
  21.4 89.6 %all-gather.6.cloned.1.call-done = bf16[64,20,3840]{2,1,0:T(8,128)(2,1)} async-done(((bf16[1,20,3840]{2,1,0:T(8,128)(2,1)}), bf16[64,20,3840]{2,1,0:T(8,128)(2,1)}) %all-gather.6.cloned.1.call-update) | async-done | bytes 9830416 | tf_op jit(solution)/shard_map/all_gather | solution.py:114
  110.9 13.6 %reshape.120 = bf16[1280,3840]{1,0:T(8,128)(2,1)} reshape(bf16[64,20,3840]{2,1,0:T(8,128)(2,1)} %all-gather.6.cloned.1.call-done) | data formatting | bytes 19660800
  124.5 7.0 %convolution_convert_fusion.1 = bf16[128,1280]{1,0:T(8,128)(2,1)S(1)} fusion(bf16[1280,3840]{1,0:T(8,128)(2,1)} %reshape.120, bf16[1,128,3840]{2,1,0:T(8,128)(2,1)S(1)} %copy-done), kind=kOutput, calls=%fused_computation.41 | convolution fusion | flops 1258455040 | bytes 11141120 | tf_op jit(solution)/shard_map/dot_general | solution.py:97
  131.6 0.9 reshape.77
  132.4 5.7 %all-to-all-start.2 = ((bf16[64,2,1280]{2,1,0:T(2,128)(2,1)}), bf16[64,2,1280]{2,1,0:T(2,128)(2,1)S(1)}, u32[]{:S(2)}, u32[]{:S(2)}) async-start(bf16[64,2,1280]{2,1,0:T(2,128)(2,1)} %reshape.77), calls=%async_computation.2 | async-start | bytes 655360 | tf_op jit(solution)/shard_map/all_to_all | solution.py:40
  138.2 2.5 sort.17
  140.9 0.9 gather_fusion
  141.8 10.5 %all-to-all-done.2 = bf16[64,2,1280]{2,1,0:T(2,128)(2,1)S(1)} async-done(((bf16[64,2,1280]{2,1,0:T(2,128)(2,1)}), bf16[64,2,1280]{2,1,0:T(2,128)(2,1)S(1)}, u32[]{:S(2)}, u32[]{:S(2)}) %all-to-all-start.2) | async-done | bytes 327712 | tf_op jit(solution)/shard_map/all_to_all | solution.py:40
  152.4 0.9 gather_fusion.2
  153.6 2.8 collective-permute-start
  156.4 1.9 collective-permute-start.1
  158.7 4.4 collective-permute-done.1
  163.6 1.8 fusion.82
  166.5 2.7 stack.111
  169.9 1.9 collective-permute-start.3
  171.8 3.8 collective-permute-start.2
  176.6 1.1 collective-permute-done.2
  178.3 2.5 add_convert_fusion
  180.9 1.7 gather_fusion.3
  182.6 3.6 fusion.83
  186.3 1.0 gather_fusion.1
  188.1 0.8 reshape.75
  188.9 15.9 %all-to-all-start.1 = ((bf16[64,2,1280]{2,1,0:T(2,128)(2,1)}), bf16[64,2,1280]{2,1,0:T(2,128)(2,1)S(1)}, u32[]{:S(2)}, u32[]{:S(2)}) async-start(bf16[64,2,1280]{2,1,0:T(2,128)(2,1)} %reshape.75), calls=%async_computation.1 | async-start | bytes 655360 | tf_op jit(solution)/shard_map/all_to_all | solution.py:51
  204.8 0.8 reshape.81
  205.6 13.7 %all-to-all-done.1 = bf16[64,2,1280]{2,1,0:T(2,128)(2,1)S(1)} async-done(((bf16[64,2,1280]{2,1,0:T(2,128)(2,1)}), bf16[64,2,1280]{2,1,0:T(2,128)(2,1)S(1)}, u32[]{:S(2)}, u32[]{:S(2)}) %all-to-all-start.1) | async-done | bytes 327712 | tf_op jit(solution)/shard_map/all_to_all | solution.py:51
  219.3 5.4 %all-to-all-start.3 = ((bf16[64,2,1280]{2,1,0:T(2,128)(2,1)}), bf16[64,2,1280]{2,1,0:T(2,128)(2,1)S(1)}, u32[]{:S(2)}, u32[]{:S(2)}) async-start(bf16[64,2,1280]{2,1,0:T(2,128)(2,1)} %reshape.81), calls=%async_computation.3 | async-start | bytes 655360 | tf_op jit(solution)/shard_map/all_to_all | solution.py:51
  224.9 16.3 %all-to-all-done.3 = bf16[64,2,1280]{2,1,0:T(2,128)(2,1)S(1)} async-done(((bf16[64,2,1280]{2,1,0:T(2,128)(2,1)}), bf16[64,2,1280]{2,1,0:T(2,128)(2,1)S(1)}, u32[]{:S(2)}, u32[]{:S(2)}) %all-to-all-start.3) | async-done | bytes 327712 | tf_op jit(solution)/shard_map/all_to_all | solution.py:51
  242.0 6.3 %fusion = bf16[1,128,3840]{2,1,0:T(8,128)(2,1)} fusion(bf16[128,1280]{1,0:T(8,128)(2,1)S(1)} %reshape.76, bf16[1280,3840]{1,0:T(8,128)(2,1)} %reshape.120), kind=kOutput, calls=%fused_computation.37 | convolution fusion | flops 1258782720 | bytes 11141120 | tf_op jit(solution)/shard_map/dot_general | solution.py:112
  248.4 174.0 %all-gather.8.cloned.1.call-done = f32[512,27,1280]{2,1,0:T(8,128)} async-done(((f32[1,27,1280]{2,1,0:T(8,128)}), f32[512,27,1280]{2,1,0:T(8,128)}) %all-gather.8.cloned.1.call-update) | async-done | bytes 70778896 | tf_op jit(solution)/shard_map/all_gather | solution.py:118
  422.3 26.7 %reduce_sum.279 = f32[27,1280]{1,0:T(8,128)} reduce(f32[512,27,1280]{2,1,0:T(8,128)} %all-gather.8.cloned.1.call-done, f32[]{:T(128)} %constant.2.clone.1), dimensions={0}, to_apply=%region_28.30 | reduce | flops 17660160 | bytes 70917120 | tf_op jit(solution)/shard_map/reduce_sum | solution.py:118
  (92 shorter events, 6.8 us)
Async XLA Ops:
  7.2 117.4 %copy-start = (bf16[1,128,3840]{2,1,0:T(8,128)(2,1)S(1)}, bf16[1,128,3840]{2,1,0:T(8,128)(2,1)}, u32[]{:S(2)}) copy-start(bf16[1,128,3840]{2,1,0:T(8,128)(2,1)} %param.11) | copy-start | bytes 2949124
  7.2 103.8 %all-gather.6.cloned.1.call-start = ((), (), s32[]{:S(2)}) async-start(), calls=%async_computation.4 | async-start | bytes 11980800 | tf_op jit(solution)/shard_map/all_gather | solution.py:114
  9.7 122.7 %all-to-all-start = ((bf16[64,2,1280]{2,1,0:T(2,128)(2,1)}), bf16[64,2,1280]{2,1,0:T(2,128)(2,1)S(1)}, u32[]{:S(2)}, u32[]{:S(2)}) async-start(bf16[64,2,1280]{2,1,0:T(2,128)(2,1)} %reshape_squeeze.3), calls=%async_computation | async-start | bytes 655360 | tf_op jit(solution)/shard_map/all_to_all | solution.py:40
  124.5 13.7 %copy-start.18 = (s32[1,128]{1,0:T(1,128)S(1)}, s32[1,128]{1,0:T(1,128)}, u32[]{:S(2)}) copy-start(s32[1,128]{1,0:T(1,128)} %param.8) | copy-start | bytes 1540
  132.4 19.9 %all-to-all-start.2 = ((bf16[64,2,1280]{2,1,0:T(2,128)(2,1)}), bf16[64,2,1280]{2,1,0:T(2,128)(2,1)S(1)}, u32[]{:S(2)}, u32[]{:S(2)}) async-start(bf16[64,2,1280]{2,1,0:T(2,128)(2,1)} %reshape.77), calls=%async_computation.2 | async-start | bytes 655360 | tf_op jit(solution)/shard_map/all_to_all | solution.py:40
  138.1 284.2 %all-gather.8.cloned.1.call-start = ((), (), s32[]{:S(2)}) async-start(), calls=%async_computation.5 | async-start | bytes 84049920 | tf_op jit(solution)/shard_map/all_gather | solution.py:118
  153.6 11.9 %copy-start.1 = (bf16[128,1280]{1,0:T(8,128)(2,1)}, bf16[128,1280]{1,0:T(8,128)(2,1)S(1)}, u32[]{:S(2)}) copy-start(bf16[128,1280]{1,0:T(8,128)(2,1)S(1)} %get-tuple-element.67) | copy-start | bytes 983044
  153.6 5.0 %collective-permute-start = (bf16[1,8,8,1280]{3,2,1,0:T(8,128)(2,1)S(1)}, bf16[1,8,8,1280]{3,2,1,0:T(8,128)(2,1)S(1)}, u32[]{:S(2)}, u32[]{:S(2)}) collective-permute-start(bf16[1,8,8,1280]{3,2,1,0:T(8,128)(2,1)S(1)} %get-tuple-element.71), channel_id=1, source_target_pairs={{0,1},{1,2},{2,3},{3,4},{4,5},{5,6},{6,7},{7,8},{8,9},{9,10},{10,1... | collective-permute-start | bytes 491528 | tf_op jit(solution)/shard_map/ppermute | solution.py:17
  156.4 6.6 %collective-permute-start.1 = (bf16[1,8,8,1280]{3,2,1,0:T(8,128)(2,1)S(1)}, bf16[1,8,8,1280]{3,2,1,0:T(8,128)(2,1)S(1)}, u32[]{:S(2)}, u32[]{:S(2)}) collective-permute-start(bf16[1,8,8,1280]{3,2,1,0:T(8,128)(2,1)S(1)} %get-tuple-element.70), channel_id=1, source_target_pairs={{1,0},{2,1},{3,2},{4,3},{5,4},{6,5},{7,6},{8,7},{9,8},{10,9},{11,1... | collective-permute-start | bytes 491528 | tf_op jit(solution)/shard_map/ppermute | solution.py:18
  163.1 2.4 copy-start.2
  165.5 3.7 copy-start.4
  169.3 11.5 %copy-start.10 = (f32[1280]{0:T(1024)}, f32[1280]{0:T(1024)S(1)}, u32[]{:S(2)}) copy-start(f32[1280]{0:T(1024)S(1)} %get-tuple-element.57) | copy-start | bytes 15364
  169.3 11.5 %copy-start.11 = (f32[1280]{0:T(1024)}, f32[1280]{0:T(1024)S(1)}, u32[]{:S(2)}) copy-start(f32[1280]{0:T(1024)S(1)} %get-tuple-element.58) | copy-start | bytes 15364
  169.3 11.5 %copy-start.12 = (f32[1280]{0:T(1024)}, f32[1280]{0:T(1024)S(1)}, u32[]{:S(2)}) copy-start(f32[1280]{0:T(1024)S(1)} %get-tuple-element.59) | copy-start | bytes 15364
  169.3 11.5 %copy-start.13 = (f32[1280]{0:T(1024)}, f32[1280]{0:T(1024)S(1)}, u32[]{:S(2)}) copy-start(f32[1280]{0:T(1024)S(1)} %get-tuple-element.60) | copy-start | bytes 15364
  169.3 11.5 %copy-start.14 = (f32[1280]{0:T(1024)}, f32[1280]{0:T(1024)S(1)}, u32[]{:S(2)}) copy-start(f32[1280]{0:T(1024)S(1)} %get-tuple-element.61) | copy-start | bytes 15364
  169.3 11.5 %copy-start.15 = (f32[1280]{0:T(1024)}, f32[1280]{0:T(1024)S(1)}, u32[]{:S(2)}) copy-start(f32[1280]{0:T(1024)S(1)} %get-tuple-element.62) | copy-start | bytes 15364
  169.3 11.5 %copy-start.16 = (f32[1280]{0:T(1024)}, f32[1280]{0:T(1024)S(1)}, u32[]{:S(2)}) copy-start(f32[1280]{0:T(1024)S(1)} %get-tuple-element.63) | copy-start | bytes 15364
  169.3 11.5 %copy-start.17 = (f32[1280]{0:T(1024)}, f32[1280]{0:T(1024)S(1)}, u32[]{:S(2)}) copy-start(f32[1280]{0:T(1024)S(1)} %get-tuple-element.64) | copy-start | bytes 15364
  169.9 6.7 %collective-permute-start.3 = (bf16[1,8,8,1280]{3,2,1,0:T(8,128)(2,1)S(1)}, bf16[1,8,8,1280]{3,2,1,0:T(8,128)(2,1)S(1)}, u32[]{:S(2)}, u32[]{:S(2)}) collective-permute-start(bf16[1,8,8,1280]{3,2,1,0:T(8,128)(2,1)S(1)} %get-tuple-element.69), channel_id=1, source_target_pairs={{1,0},{2,1},{3,2},{4,3},{5,4},{6,5},{7,6},{8,7},{9,8},{10,9},{11,1... | collective-permute-start | bytes 491528 | tf_op jit(solution)/shard_map/ppermute | solution.py:18
  171.8 5.9 %collective-permute-start.2 = (bf16[1,8,8,1280]{3,2,1,0:T(8,128)(2,1)S(1)}, bf16[1,8,8,1280]{3,2,1,0:T(8,128)(2,1)S(1)}, u32[]{:S(2)}, u32[]{:S(2)}) collective-permute-start(bf16[1,8,8,1280]{3,2,1,0:T(8,128)(2,1)S(1)} %get-tuple-element.68), channel_id=1, source_target_pairs={{0,1},{1,2},{2,3},{3,4},{4,5},{5,6},{6,7},{7,8},{8,9},{9,10},{10,1... | collective-permute-start | bytes 491528 | tf_op jit(solution)/shard_map/ppermute | solution.py:17
  176.5 4.3 copy-start.5
  176.5 4.3 copy-start.6
  176.6 4.3 copy-start.7
  176.6 4.3 copy-start.8
  176.6 4.3 copy-start.9
  182.6 4.7 %copy-start.3 = (bf16[128,1280]{1,0:T(8,128)(2,1)S(1)}, bf16[128,1280]{1,0:T(8,128)(2,1)}, u32[]{:S(2)}) copy-start(bf16[128,1280]{1,0:T(8,128)(2,1)} %gather_fusion.3) | copy-start | bytes 983044
  188.9 30.4 %all-to-all-start.1 = ((bf16[64,2,1280]{2,1,0:T(2,128)(2,1)}), bf16[64,2,1280]{2,1,0:T(2,128)(2,1)S(1)}, u32[]{:S(2)}, u32[]{:S(2)}) async-start(bf16[64,2,1280]{2,1,0:T(2,128)(2,1)} %reshape.75), calls=%async_computation.1 | async-start | bytes 655360 | tf_op jit(solution)/shard_map/all_to_all | solution.py:51
  219.3 21.9 %all-to-all-start.3 = ((bf16[64,2,1280]{2,1,0:T(2,128)(2,1)}), bf16[64,2,1280]{2,1,0:T(2,128)(2,1)S(1)}, u32[]{:S(2)}, u32[]{:S(2)}) async-start(bf16[64,2,1280]{2,1,0:T(2,128)(2,1)} %reshape.81), calls=%async_computation.3 | async-start | bytes 655360 | tf_op jit(solution)/shard_map/all_to_all | solution.py:51
Sparse Core Ops, SparseCore 0:
  11.3 99.6 all-gather.5
  169.3 253.0 all-gather.7
